TPU v7x, 32 devices: a whole 2x2x4 slice. The times are simulated.
32 devices in a mesh: ta: 16 (over z, x, core), pa: 2 (over y).
Axes of the slice: x: 2, y: 2, z: 4, core: 2. Of those that a mesh axis runs over, the one named last changes fastest.
Arguments:
- occupied_orbitals: bfloat16 [4096, 512], P('pa'), may hold values from -3 to 3
- virtual_orbitals: bfloat16 [4096, 1536], P('pa'), may hold values from -2.5 to 2.5
- occupied_gaps: float32 [512], replicated, may hold values from 0.05 to 2
- virtual_gaps: float32 [1536], replicated, may hold values from 0.05 to 2
- tile_columns: int32 [32, 8], replicated, may hold values from 0 to 31, as said below
- probe_vectors: bfloat16 [32, 4096], P(None, 'ta'), may hold values from -0.1875 to 0.1875
Outputs:
- response: float32 [16, 32, 4096], P('ta', None, 'pa')
Inputs may be any that keep to these rules, and one draw needn't show every extreme that they name: `tile_columns`: each row block lists 8 different column blocks, and every column block is listed by some row block.
All inputs are finite; a program needn't handle non-finite values.
Results may differ from a plain program's by a relative error of at most 0.00083.
Values may be sent and summed in bfloat16 or wider, within the bound.
No kernel may reach another device: no remote copies, remote signals or barrier semaphores. Data moves between devices by JAX's collectives and lax.ppermute only.
A program may use at most 128 MiB of HBM per device.

v0:
```python
import functools

import jax
import jax.numpy as jnp
from jax import lax
from jax.experimental import pallas as pl
from jax.experimental.pallas import tpu as pltpu
from jax.sharding import PartitionSpec as P

BLK = 128
NT = 32
NVEC = 32
VMEM_BYTES = 52 * 2**20
NT_DIMS = (((1,), (1,)), ((), ()))
ANY = pl.BlockSpec(memory_space=pl.ANY)
SMEM = pl.BlockSpec(memory_space=pltpu.SMEM)
VMEM = pl.BlockSpec(memory_space=pltpu.VMEM)


def quadrature_grids(count_times, count_freqs):
    low_time = jnp.log(jnp.float32(0.05))
    high_time = jnp.log(jnp.float32(8.0))
    time_place = (jnp.arange(count_times, dtype=jnp.float32) + 0.5) / count_times
    times_grid = jnp.exp(low_time + (high_time - low_time) * time_place)
    weights_grid = times_grid * (high_time - low_time) / count_times
    low_freq = jnp.log(jnp.float32(0.05))
    high_freq = jnp.log(jnp.float32(20.0))
    freq_place = (jnp.arange(count_freqs, dtype=jnp.float32) + 0.5) / count_freqs
    freqs_grid = jnp.exp(low_freq + (high_freq - low_freq) * freq_place)
    cosine_table = 2.0 * weights_grid[None, :] * jnp.cos(freqs_grid[:, None] * times_grid[None, :])
    return (times_grid, cosine_table)


class Plan:
    def __init__(self, panels, tiles, blocks):
        self.panels = panels
        self.tiles = tiles
        self.blocks = blocks
        self.cols = panels
        self.order = panels + panels * tiles
        self.size = self.order + blocks


def prep_kernel(plan, group, tiles_ref, probe, occ, virt, out, sent, spread, costs, ranked, sems):
    panels, tiles, blocks = plan.panels, plan.tiles, plan.blocks
    here = lax.axis_index("pa")
    slot = lax.div(lax.axis_index("ta"), jnp.int32(group))
    virt_count = virt.shape[1]
    place = pl.ds(pl.multiple_of(slot * BLK, BLK), BLK)
    copy_virt = pltpu.make_async_copy(
        virt.at[place, :], sent.at[:, pl.ds(0, virt_count)], sems.at[0]
    )
    copy_occ = pltpu.make_async_copy(
        occ.at[place, :], sent.at[:, pl.ds(virt_count, occ.shape[1])], sems.at[1]
    )
    copy_virt.start()
    copy_occ.start()

    width = spread.shape[3]
    for piece in range(spread.shape[1]):
        value = probe[:, piece * width : (piece + 1) * width]
        for target in range(spread.shape[0]):
            spread[target, piece] = value

    low = here * blocks

    def inside(row, k):
        column = tiles_ref[row, k]
        return ((column >= low) & (column < low + blocks)).astype(jnp.int32)

    def count(row):
        total = jnp.int32(0)
        for k in range(tiles):
            total += inside(row, k)
        return total

    def one_cost(s, carry):
        costs[s] = count(low + s)
        total = jnp.int32(0)
        for offset in range(1, panels):
            total += count(lax.rem(here + offset, panels) * blocks + s)
        costs[blocks + s] = total
        return carry

    lax.fori_loop(0, blocks, one_cost, 0)

    def rank_own(s, carry):
        mine = costs[s]
        rank = jnp.int32(0)
        for j in range(blocks):
            other = costs[j]
            rank += ((other < mine) | ((other == mine) & (j < s))).astype(jnp.int32)
        ranked[rank] = s
        return carry

    lax.fori_loop(0, blocks, rank_own, 0)

    def rank_other(s, carry):
        mine = costs[blocks + s]
        rank = jnp.int32(0)
        for j in range(blocks):
            other = costs[blocks + j]
            rank += ((other > mine) | ((other == mine) & (j < s))).astype(jnp.int32)
        out[plan.order + s] = ranked[rank]
        return carry

    lax.fori_loop(0, blocks, rank_other, 0)

    for which in range(panels):
        if which < panels - 1:
            row = lax.rem(here + which + 1, panels) * blocks + slot
        else:
            row = low + out[plan.order + slot]
        total = jnp.int32(0)
        for k in range(tiles):
            out[plan.cols + which * tiles + total] = tiles_ref[row, k] - low
            total += inside(row, k)
        out[which] = total

    copy_virt.wait()
    copy_occ.wait()


def scale_rows(times, gaps_occ, gaps_virt, row_occ, row_virt, scaled_occ, scaled_virt):
    def one_time(t, carry):
        place = pl.ds(pl.multiple_of(t * BLK, BLK), BLK)
        minus_time = -times[t]
        for gaps, row, scaled in (
            (gaps_occ, row_occ, scaled_occ),
            (gaps_virt, row_virt, scaled_virt),
        ):
            weights = jnp.exp(minus_time * gaps[...].reshape(1, -1))
            scaled[place, :] = (row[...].astype(jnp.float32) * weights).astype(jnp.bfloat16)
        return carry

    lax.fori_loop(0, scaled_occ.shape[0] // BLK, one_time, 0)


def loaded_tiles(count):
    return jnp.where(count == 1, 2, count)


def tile_copies(plan, table, which, tile, occ, virt, cols_occ, cols_virt, sems):
    last = jnp.maximum(table[which] - 1, 0)
    column = table[plan.cols + which * plan.tiles + jnp.minimum(tile, last)]
    source = pl.ds(pl.multiple_of(column * BLK, BLK), BLK)
    target = pl.ds(pl.multiple_of(tile * BLK, BLK), BLK)
    return (
        pltpu.make_async_copy(occ.at[source, :], cols_occ.at[target, :], sems.at[0, tile]),
        pltpu.make_async_copy(virt.at[source, :], cols_virt.at[target, :], sems.at[1, tile]),
    )


def over_groups(count, one_group):
    triple = (lax.rem(count, 2) == 1) & (count >= 3)
    pairs = lax.div(loaded_tiles(count), 2) - triple.astype(jnp.int32)

    def one_pair(g, carry):
        one_group(2 * g, 2)
        return carry

    lax.fori_loop(0, pairs, one_pair, 0)

    @pl.when(triple)
    def _():
        one_group(2 * pairs, 3)


def polar_chunk(columns, place, scaled_occ, scaled_virt, cols_occ, cols_virt):
    green_occ = lax.dot_general(
        cols_occ[columns, :], scaled_occ[place, :], NT_DIMS, preferred_element_type=jnp.float32
    )
    green_virt = lax.dot_general(
        cols_virt[columns, :], scaled_virt[place, :], NT_DIMS, preferred_element_type=jnp.float32
    )
    return (green_occ * green_virt).astype(jnp.bfloat16)


def start_tiles(copies, count):
    def one_tile(tile, carry):
        for copy in copies(tile):
            copy.start()
        return carry

    lax.fori_loop(0, loaded_tiles(count), one_tile, 0)


def own_kernel(
    plan, chunk, table, times, gaps_occ, gaps_virt, occ, virt, polar,
    row_occ, row_virt, scaled_occ, scaled_virt, cols_occ, cols_virt, kept,
    row_sems, tile_sems, out_sems,
):
    which = plan.panels - 1
    slot = lax.div(lax.axis_index("ta"), jnp.int32(lax.axis_size("ta") // plan.blocks))
    own = table[plan.order + slot]
    count = table[which]
    rows = scaled_occ.shape[0]
    place = pl.ds(pl.multiple_of(own * BLK, BLK), BLK)
    row_copies = (
        pltpu.make_async_copy(occ.at[place, :], row_occ, row_sems.at[0]),
        pltpu.make_async_copy(virt.at[place, :], row_virt, row_sems.at[1]),
    )
    copies = lambda tile: tile_copies(
        plan, table, which, tile, occ, virt, cols_occ, cols_virt, tile_sems
    )
    for copy in row_copies:
        copy.start()
    start_tiles(copies, count)
    for copy in row_copies:
        copy.wait()
    scale_rows(times, gaps_occ, gaps_virt, row_occ, row_virt, scaled_occ, scaled_virt)

    def saved(first, size, i):
        columns = pl.ds(pl.multiple_of(first * BLK, BLK), size * BLK)
        part = pl.ds(pl.multiple_of(i * chunk, chunk), chunk)
        return pltpu.make_async_copy(
            kept.at[columns, part], polar.at[columns, part], out_sems.at[first, i]
        )

    def compute(first, size):
        for tile in range(size):
            for copy in copies(first + tile):
                copy.wait()
        columns = pl.ds(pl.multiple_of(first * BLK, BLK), size * BLK)

        def one_chunk(i, carry):
            part = pl.ds(pl.multiple_of(i * chunk, chunk), chunk)
            kept[columns, part] = polar_chunk(
                columns, part, scaled_occ, scaled_virt, cols_occ, cols_virt
            )
            saved(first, size, i).start()
            return carry

        lax.fori_loop(0, rows // chunk, one_chunk, 0)

    def finish(first, size):
        def one_chunk(i, carry):
            saved(first, size, i).wait()
            return carry

        lax.fori_loop(0, rows // chunk, one_chunk, 0)

    over_groups(count, compute)
    over_groups(count, finish)


def rest_kernel(
    plan, chunk, table, times, cosine, gaps_occ, gaps_virt, other_rows, occ, virt, polar, probes,
    out, row_occ, row_virt, scaled_occ, scaled_virt, cols_occ, cols_virt, kept, terms,
    probe_two, probe_three, row_sems, tile_sems, kept_sems,
):
    panels = plan.panels
    here = lax.axis_index("pa")
    rows = scaled_occ.shape[0]
    virt_count = virt.shape[1]
    own_count = table[panels - 1]

    def kept_copies(tile):
        place = pl.ds(pl.multiple_of(tile * BLK, BLK), BLK)
        return (
            pltpu.make_async_copy(polar.at[place, :], kept.at[place, :], kept_sems.at[tile]),
        )

    def load_probes(which, first, size):
        held = probe_two if size == 2 else probe_three
        count = table[which]
        for tile in range(size):
            at = jnp.minimum(first + tile, jnp.maximum(count - 1, 0))
            value = probes[here * plan.blocks + table[plan.cols + which * plan.tiles + at]]
            held[:, tile * BLK : (tile + 1) * BLK] = jnp.where(
                first + tile < count, value, jnp.zeros_like(value)
            )
        return held

    terms[...] = jnp.zeros_like(terms)

    def one_other(which, carry):
        count = table[which]
        place = pl.ds(pl.multiple_of(which * BLK, BLK), BLK)
        row_copies = (
            pltpu.make_async_copy(
                other_rows.at[place, pl.ds(0, virt_count)], row_virt, row_sems.at[0]
            ),
            pltpu.make_async_copy(
                other_rows.at[place, pl.ds(virt_count, occ.shape[1])], row_occ, row_sems.at[1]
            ),
        )
        copies = lambda tile: tile_copies(
            plan, table, which, tile, occ, virt, cols_occ, cols_virt, tile_sems
        )
        for copy in row_copies:
            copy.start()
        start_tiles(copies, count)

        @pl.when(which == 0)
        def _():
            start_tiles(kept_copies, own_count)

        for copy in row_copies:
            copy.wait()
        scale_rows(times, gaps_occ, gaps_virt, row_occ, row_virt, scaled_occ, scaled_virt)

        def compute(first, size):
            for tile in range(size):
                for copy in copies(first + tile):
                    copy.wait()
            held = load_probes(which, first, size)
            columns = pl.ds(pl.multiple_of(first * BLK, BLK), size * BLK)

            def one_chunk(i, carry):
                part = pl.ds(pl.multiple_of(i * chunk, chunk), chunk)
                value = polar_chunk(columns, part, scaled_occ, scaled_virt, cols_occ, cols_virt)
                terms[which, :, part] += jnp.dot(
                    held[...], value, preferred_element_type=jnp.float32
                )
                return carry

            lax.fori_loop(0, rows // chunk, one_chunk, 0)

        over_groups(count, compute)
        return carry

    lax.fori_loop(0, panels - 1, one_other, 0)

    def apply_own(first, size):
        for tile in range(size):
            for copy in kept_copies(first + tile):
                copy.wait()
        held = load_probes(panels - 1, first, size)
        columns = pl.ds(pl.multiple_of(first * BLK, BLK), size * BLK)

        def one_chunk(i, carry):
            part = pl.ds(pl.multiple_of(i * chunk, chunk), chunk)
            terms[panels - 1, :, part] += jnp.dot(
                held[...], kept[columns, part], preferred_element_type=jnp.float32
            )
            return carry

        lax.fori_loop(0, rows // chunk, one_chunk, 0)

    over_groups(own_count, apply_own)

    for which in range(panels):
        dest = lax.rem(here + which + 1, panels)

        def one_freq(k, carry):
            total = jnp.zeros((NVEC, BLK), jnp.float32)
            for t in range(rows // BLK):
                total += cosine[k, t] * terms[which, :, t * BLK : (t + 1) * BLK]
            out[k * panels + dest] = total
            return carry

        lax.fori_loop(0, out.shape[0] // panels, one_freq, 0)


def sum_kernel(plan, group, table, parts, out):
    panels, blocks = plan.panels, plan.blocks
    here = lax.axis_index("pa")
    for slot in range(blocks):
        total = jnp.zeros((NVEC, BLK), jnp.float32)
        for offset in range(1, panels):
            panel = lax.rem(here + offset, panels)
            for member in range(group):
                total += parts[(slot * group + member) * panels + panel]
        out[0, :, slot * BLK : (slot + 1) * BLK] = total
    for slot in range(blocks):
        total = parts[slot * group * panels + here]
        for member in range(1, group):
            total += parts[(slot * group + member) * panels + here]
        place = pl.ds(pl.multiple_of(table[plan.order + slot] * BLK, BLK), BLK)
        out[0, :, place] += total


def shards(
    occupied_orbitals, virtual_orbitals, occupied_gaps, virtual_gaps, tile_columns, probe_vectors
):
    count_ta = lax.axis_size("ta")
    panels = lax.axis_size("pa")
    panel_rows, occ_count = occupied_orbitals.shape
    virt_count = virtual_orbitals.shape[1]
    slice_width = probe_vectors.shape[1]
    tiles = tile_columns.shape[1]
    blocks = panel_rows // BLK
    group = count_ta // blocks
    local_times = NT // group
    rows = local_times * BLK
    chunk = min(rows, 1024)
    chunks = rows // chunk
    plan = Plan(panels, tiles, blocks)
    width = min(slice_width, BLK)
    params = pltpu.CompilerParams(vmem_limit_bytes=VMEM_BYTES)

    table, sent, spread = pl.pallas_call(
        functools.partial(prep_kernel, plan, group),
        in_specs=[SMEM, VMEM, ANY, ANY],
        out_specs=(SMEM, ANY, VMEM),
        out_shape=(
            jax.ShapeDtypeStruct((plan.size,), jnp.int32),
            jax.ShapeDtypeStruct((BLK, virt_count + occ_count), jnp.bfloat16),
            jax.ShapeDtypeStruct((count_ta, slice_width // width, NVEC, width), jnp.bfloat16),
        ),
        scratch_shapes=[
            pltpu.SMEM((2 * blocks,), jnp.int32),
            pltpu.SMEM((blocks,), jnp.int32),
            pltpu.SemaphoreType.DMA((2,)),
        ],
        compiler_params=params,
        name="prep",
    )(tile_columns, probe_vectors, occupied_orbitals, virtual_orbitals)

    others = [
        lax.ppermute(sent, "pa", [(q, (q - offset) % panels) for q in range(panels)])
        for offset in range(1, panels)
    ]
    other_rows = others[0] if panels == 2 else jnp.concatenate(others, axis=0)

    probes = lax.all_to_all(spread, "ta", 0, 0, tiled=True)
    if width < BLK:
        probes = probes.reshape(-1, BLK // width, NVEC, width).transpose(0, 2, 1, 3)
    probes = probes.reshape(-1, NVEC, BLK)

    times, cosine = quadrature_grids(NT, count_ta)
    if group > 1:
        first_time = (lax.axis_index("ta") % group) * local_times
        times = lax.dynamic_slice_in_dim(times, first_time, local_times, 0)
        cosine = lax.dynamic_slice_in_dim(cosine, first_time, local_times, 1)

    scratch = [
        pltpu.VMEM((BLK, occ_count), jnp.bfloat16),
        pltpu.VMEM((BLK, virt_count), jnp.bfloat16),
        pltpu.VMEM((rows, occ_count), jnp.bfloat16),
        pltpu.VMEM((rows, virt_count), jnp.bfloat16),
        pltpu.VMEM((tiles * BLK, occ_count), jnp.bfloat16),
        pltpu.VMEM((tiles * BLK, virt_count), jnp.bfloat16),
        pltpu.VMEM((tiles * BLK, rows), jnp.bfloat16),
    ]
    sems = [pltpu.SemaphoreType.DMA((2,)), pltpu.SemaphoreType.DMA((2, tiles))]
    cost = pl.CostEstimate(
        flops=tiles * BLK * rows * (occ_count + virt_count), bytes_accessed=2**23, transcendentals=0
    )
    polar = pl.pallas_call(
        functools.partial(own_kernel, plan, chunk),
        in_specs=[SMEM, SMEM, VMEM, VMEM, ANY, ANY],
        out_specs=ANY,
        out_shape=jax.ShapeDtypeStruct((tiles * BLK, rows), jnp.bfloat16),
        scratch_shapes=scratch + sems + [pltpu.SemaphoreType.DMA((tiles, chunks))],
        compiler_params=params,
        cost_estimate=cost,
        name="own_tiles",
    )(table, times, occupied_gaps, virtual_gaps, occupied_orbitals, virtual_orbitals)

    partial_response = pl.pallas_call(
        functools.partial(rest_kernel, plan, chunk),
        in_specs=[SMEM, SMEM, SMEM, VMEM, VMEM, ANY, ANY, ANY, ANY, VMEM],
        out_specs=VMEM,
        out_shape=jax.ShapeDtypeStruct((count_ta * panels, NVEC, BLK), jnp.float32),
        scratch_shapes=scratch
        + [
            pltpu.VMEM((panels, NVEC, rows), jnp.float32),
            pltpu.VMEM((NVEC, 2 * BLK), jnp.bfloat16),
            pltpu.VMEM((NVEC, 3 * BLK), jnp.bfloat16),
        ]
        + sems
        + [pltpu.SemaphoreType.DMA((tiles,))],
        compiler_params=params,
        cost_estimate=cost,
        name="other_tiles",
    )(
        table, times, cosine, occupied_gaps, virtual_gaps, other_rows,
        occupied_orbitals, virtual_orbitals, polar, probes,
    )

    parts = lax.all_to_all(partial_response, ("ta", "pa"), 0, 0, tiled=True)
    return pl.pallas_call(
        functools.partial(sum_kernel, plan, group),
        in_specs=[SMEM, VMEM],
        out_specs=VMEM,
        out_shape=jax.ShapeDtypeStruct((1, NVEC, panel_rows), jnp.float32),
        compiler_params=params,
        name="sum_parts",
    )(table, parts)


def solution(mesh):
    placed = (P("pa", None), P("pa", None), P(), P(), P(), P(None, "ta"))
    return jax.shard_map(
        shards, mesh=mesh, in_specs=placed, out_specs=P("ta", None, "pa"), check_vma=False
    )
```

profile of v0, /device:TPU:1, one launch (start us, length us, event | category | flops | bytes accessed | tf_op | source)
XLA Modules:
  0.0 73.1 jit_solution(16648439130526734411)
XLA Ops:
  0.0 0.0 copy-start.1
  0.0 0.0 copy-start.2
  0.0 0.8 %copy.7.tiles_ref = s32[32,8]{1,0:T(8,128)S(1)} copy(s32[32,8]{0,1:T(8,128)} %param.10) | data formatting | bytes 2048 | tf_op args[4]
  0.8 0.0 copy-start
  0.8 0.7 copy-done
  1.5 3.9 %prep.1 = (s32[34]{0:T(128)S(1)}, bf16[128,2048]{1,0:T(8,128)(2,1)S(1)}, bf16[16,2,32,128]{3,2,1,0:T(8,128)(2,1)}) custom-call(s32[32,8]{1,0:T(8,128)S(1)} %copy.7.tiles_ref, bf16[32,256]{1,0:T(8,128)(2,1)S(1)} %copy-done, bf16[2048,512]{1,0:T(8,128)(2,1)} %occ.5, bf16[2048,1536]{1,0:T(8,128)(2,1)} %virt.5), custom_call_target="tpu_custom_call" | custom-call | tf_op jit(solution)/shard_map/prep/pallas_call | solution.py:393
  5.4 7.3 %all-to-all-start = ((bf16[16,2,32,128]{3,2,1,0:T(8,128)(2,1)}), bf16[16,2,32,128]{3,2,1,0:T(8,128)(2,1)S(1)}, u32[]{:S(2)}, u32[]{:S(2)}) async-start(bf16[16,2,32,128]{3,2,1,0:T(8,128)(2,1)} %get-tuple-element.10), calls=%async_computation | async-start | bytes 524288 | tf_op jit(solution)/shard_map/all_to_all | solution.py:417
  12.7 1.2 %collective-permute-start = (bf16[128,2048]{1,0:T(8,128)(2,1)S(1)}, bf16[128,2048]{1,0:T(8,128)(2,1)S(1)}, u32[]{:S(2)}, u32[]{:S(2)}) collective-permute-start(bf16[128,2048]{1,0:T(8,128)(2,1)S(1)} %get-tuple-element.9), channel_id=1, source_target_pairs={{0,1},{1,0},{2,3},{3,2},{4,5},{5,4},{6,7},{7,6},{8,9},{9,8},{10,11... | collective-permute-start | bytes 1572872 | tf_op jit(solution)/shard_map/ppermute | solution.py:412
  14.0 0.0 copy-done.1
  14.0 0.0 copy-done.2
  14.0 18.4 %own_tiles.1.polar = bf16[1024,4096]{1,0:T(8,128)(2,1)} custom-call(s32[34]{0:T(128)S(1)} %get-tuple-element.8.table, f32[32]{0:T(128)S(1)} %get-tuple-element.11.times, f32[512]{0:T(512)S(1)} %copy-done.2, f32[1536]{0:T(1024)S(1)} %copy-done.1, bf16[2048,512]{1,0:T(8,128)(2,1)} %occ.5, bf16[2048,1536]{1,0:T(8,128)(2,1)} %virt.5), custom_call_target="tpu_custom_call" | custom-call | flops 8589934592 | bytes 8388608 | tf_op jit(solution)/shard_map/own_tiles/pallas_call | solution.py:441
  32.5 0.1 cosine_multiply_fusion.cosine
  32.6 0.0 all-to-all-done
  32.6 0.0 collective-permute-done.other_rows
  32.6 19.2 %other_tiles.1 = f32[32,32,128]{2,1,0:T(8,128)S(1)} custom-call(s32[34]{0:T(128)S(1)} %get-tuple-element.8.table, f32[32]{0:T(128)S(1)} %get-tuple-element.11.times, f32[16,32]{1,0:T(8,128)S(1)} %cosine_multiply_fusion.cosine, f32[512]{0:T(512)S(1)} %copy-done.2, f32[1536]{0:T(1024)S(1)} %copy-done.1, bf16[128,2048]{1,0:T(8,128)(2,1)S(1)} %collective-permute-done.other_rows, ...), custom_call_target="tpu_custom_call" | custom-call | flops 8589934592 | bytes 8388608 | tf_op jit(solution)/shard_map/other_tiles/pallas_call | solution.py:452
  51.9 19.9 %all_to_all.10.parts = f32[32,32,128]{2,1,0:T(8,128)S(1)} all-to-all(f32[32,32,128]{2,1,0:T(8,128)S(1)} %other_tiles.1), channel_id=1, replica_groups=mesh['ta'=16,'pa'=2] {'ta','pa'}, dimensions={0} | all-to-all | bytes 1048576 | tf_op jit(solution)/shard_map/all_to_all | solution.py:473
  71.8 1.3 %sum_parts.1 = f32[1,32,2048]{2,1,0:T(8,128)} custom-call(s32[34]{0:T(128)S(1)} %get-tuple-element.8.table, f32[32,32,128]{2,1,0:T(8,128)S(1)} %all_to_all.10.parts), custom_call_target="tpu_custom_call" | custom-call | tf_op jit(solution)/shard_map/sum_parts/pallas_call | solution.py:474
  (2 shorter events, 0.0 us)
Async XLA Ops:
  0.0 14.0 %copy-start.1 = (f32[1536]{0:T(1024)S(1)}, f32[1536]{0:T(1024)}, u32[]{:S(2)}) copy-start(f32[1536]{0:T(1024)} %gaps_virt.3) | copy-start | bytes 18436
  0.0 14.0 %copy-start.2 = (f32[512]{0:T(512)S(1)}, f32[512]{0:T(512)}, u32[]{:S(2)}) copy-start(f32[512]{0:T(512)} %gaps_occ.3) | copy-start | bytes 6148
  0.8 0.7 copy-start
  5.4 27.2 %all-to-all-start = ((bf16[16,2,32,128]{3,2,1,0:T(8,128)(2,1)}), bf16[16,2,32,128]{3,2,1,0:T(8,128)(2,1)S(1)}, u32[]{:S(2)}, u32[]{:S(2)}) async-start(bf16[16,2,32,128]{3,2,1,0:T(8,128)(2,1)} %get-tuple-element.10), calls=%async_computation | async-start | bytes 524288 | tf_op jit(solution)/shard_map/all_to_all | solution.py:417
  12.7 19.9 %collective-permute-start = (bf16[128,2048]{1,0:T(8,128)(2,1)S(1)}, bf16[128,2048]{1,0:T(8,128)(2,1)S(1)}, u32[]{:S(2)}, u32[]{:S(2)}) collective-permute-start(bf16[128,2048]{1,0:T(8,128)(2,1)S(1)} %get-tuple-element.9), channel_id=1, source_target_pairs={{0,1},{1,0},{2,3},{3,2},{4,5},{5,4},{6,7},{7,6},{8,9},{9,8},{10,11... | collective-permute-start | bytes 1572872 | tf_op jit(solution)/shard_map/ppermute | solution.py:412
where the time goes:
time: 74 us; the launch traced here: 73.1 us
  Pallas kernels  42.9 us (58%)
  blocking collectives  19.9 us (27%)
  starting transfers between devices  8.57 us (12%)
  local copies, waits for them, and re-layouts  1.51 us (2%)
    all_to_all x1, blocking collectives, shards(): parts = lax.all_to_all(partial_response, ('ta', 'pa'), 0, 0, tiled=True)  19.9 us
    pallas_call x1, Pallas kernels, shards(): pl.pallas_call(functools.partial(rest_kernel, plan, chunk), in_specs=[SME...  19.2 us
    pallas_call x1, Pallas kernels, shards(): pl.pallas_call(functools.partial(own_kernel, plan, chunk), in_specs=[SMEM...  18.4 us
    all_to_all x1, starting transfers between devices, shards(): probes = lax.all_to_all(spread, 'ta', 0, 0, tiled=True)  7.33 us
    pallas_call x1, Pallas kernels, shards(): pl.pallas_call(functools.partial(prep_kernel, plan, group), in_specs=[SME...  3.89 us
    unnamed x7, local copies, waits for them, and re-layouts  1.51 us
  transfers between devices with their start and end apart: 2, of which 0 were waited for; matrix products, arithmetic and copies ran while one was open for 0% of the time, Pallas kernels for 25%

commit v1 on v0

--- a/solution.py
+++ b/solution.py
@@ -10,6 +10,7 @@
 BLK = 128
 NT = 32
 NVEC = 32
+FREQS = 4
 VMEM_BYTES = 52 * 2**20
 NT_DIMS = (((1,), (1,)), ((), ()))
 ANY = pl.BlockSpec(memory_space=pl.ANY)
@@ -41,31 +42,36 @@
         self.size = self.order + blocks
 
 
-def prep_kernel(plan, group, tiles_ref, probe, occ, virt, out, sent, spread, costs, ranked, sems):
+def pack_kernel(group, occ, virt, sent, sems):
+    slot = lax.div(lax.axis_index("ta"), jnp.int32(group))
+    virt_count = virt.shape[1]
+    place = pl.ds(pl.multiple_of(slot * BLK, BLK), BLK)
+    copies = (
+        pltpu.make_async_copy(virt.at[place, :], sent.at[:, pl.ds(0, virt_count)], sems.at[0]),
+        pltpu.make_async_copy(
+            occ.at[place, :], sent.at[:, pl.ds(virt_count, occ.shape[1])], sems.at[1]
+        ),
+    )
+    for copy in copies:
+        copy.start()
+    for copy in copies:
+        copy.wait()
+
+
+def plan_kernel(plan, group, tiles_hbm, probe_hbm, after, out, spread, listed, probe, keys, ranked, sems):
     panels, tiles, blocks = plan.panels, plan.tiles, plan.blocks
     here = lax.axis_index("pa")
     slot = lax.div(lax.axis_index("ta"), jnp.int32(group))
-    virt_count = virt.shape[1]
-    place = pl.ds(pl.multiple_of(slot * BLK, BLK), BLK)
-    copy_virt = pltpu.make_async_copy(
-        virt.at[place, :], sent.at[:, pl.ds(0, virt_count)], sems.at[0]
-    )
-    copy_occ = pltpu.make_async_copy(
-        occ.at[place, :], sent.at[:, pl.ds(virt_count, occ.shape[1])], sems.at[1]
-    )
-    copy_virt.start()
-    copy_occ.start()
-
-    width = spread.shape[3]
-    for piece in range(spread.shape[1]):
-        value = probe[:, piece * width : (piece + 1) * width]
-        for target in range(spread.shape[0]):
-            spread[target, piece] = value
+    copy_tiles = pltpu.make_async_copy(tiles_hbm, listed, sems.at[0])
+    copy_probe = pltpu.make_async_copy(probe_hbm, probe, sems.at[1])
+    copy_tiles.start()
+    copy_probe.start()
+    copy_tiles.wait()
 
     low = here * blocks
 
     def inside(row, k):
-        column = tiles_ref[row, k]
+        column = listed[row, k]
         return ((column >= low) & (column < low + blocks)).astype(jnp.int32)
 
     def count(row):
@@ -75,36 +81,29 @@
         return total
 
     def one_cost(s, carry):
-        costs[s] = count(low + s)
         total = jnp.int32(0)
         for offset in range(1, panels):
             total += count(lax.rem(here + offset, panels) * blocks + s)
-        costs[blocks + s] = total
+        keys[0, s] = count(low + s) * blocks + s
+        keys[1, s] = s - total * blocks
         return carry
 
     lax.fori_loop(0, blocks, one_cost, 0)
 
-    def rank_own(s, carry):
-        mine = costs[s]
-        rank = jnp.int32(0)
+    def one_rank(s, carry):
+        own, other = keys[0, s], keys[1, s]
+        own_rank = jnp.int32(0)
+        other_rank = jnp.int32(0)
         for j in range(blocks):
-            other = costs[j]
-            rank += ((other < mine) | ((other == mine) & (j < s))).astype(jnp.int32)
-        ranked[rank] = s
+            own_rank += (keys[0, j] < own).astype(jnp.int32)
+            other_rank += (keys[1, j] < other).astype(jnp.int32)
+        ranked[0, own_rank] = s
+        ranked[1, other_rank] = s
         return carry
 
-    lax.fori_loop(0, blocks, rank_own, 0)
-
-    def rank_other(s, carry):
-        mine = costs[blocks + s]
-        rank = jnp.int32(0)
-        for j in range(blocks):
-            other = costs[blocks + j]
-            rank += ((other > mine) | ((other == mine) & (j < s))).astype(jnp.int32)
-        out[plan.order + s] = ranked[rank]
-        return carry
-
-    lax.fori_loop(0, blocks, rank_other, 0)
+    lax.fori_loop(0, blocks, one_rank, 0)
+    for rank in range(blocks):
+        out[plan.order + ranked[1, rank]] = ranked[0, rank]
 
     for which in range(panels):
         if which < panels - 1:
@@ -113,12 +112,16 @@
             row = low + out[plan.order + slot]
         total = jnp.int32(0)
         for k in range(tiles):
-            out[plan.cols + which * tiles + total] = tiles_ref[row, k] - low
+            out[plan.cols + which * tiles + total] = listed[row, k] - low
             total += inside(row, k)
         out[which] = total
 
-    copy_virt.wait()
-    copy_occ.wait()
+    copy_probe.wait()
+    width = spread.shape[3]
+    for piece in range(spread.shape[1]):
+        value = probe[:, piece * width : (piece + 1) * width]
+        for target in range(spread.shape[0]):
+            spread[target, piece] = value
 
 
 def scale_rows(times, gaps_occ, gaps_virt, row_occ, row_virt, scaled_occ, scaled_virt):
@@ -343,14 +346,17 @@
     for which in range(panels):
         dest = lax.rem(here + which + 1, panels)
 
-        def one_freq(k, carry):
-            total = jnp.zeros((NVEC, BLK), jnp.float32)
+        def some_freqs(g, carry):
+            totals = [jnp.zeros((NVEC, BLK), jnp.float32)] * FREQS
             for t in range(rows // BLK):
-                total += cosine[k, t] * terms[which, :, t * BLK : (t + 1) * BLK]
-            out[k * panels + dest] = total
+                value = terms[which, :, t * BLK : (t + 1) * BLK]
+                for j in range(FREQS):
+                    totals[j] += cosine[g * FREQS + j, t] * value
+            for j in range(FREQS):
+                out[(g * FREQS + j) * panels + dest] = totals[j]
             return carry
 
-        lax.fori_loop(0, out.shape[0] // panels, one_freq, 0)
+        lax.fori_loop(0, out.shape[0] // (panels * FREQS), some_freqs, 0)
 
 
 def sum_kernel(plan, group, table, parts, out):
@@ -384,29 +390,39 @@
     group = count_ta // blocks
     local_times = NT // group
     rows = local_times * BLK
-    chunk = min(rows, 1024)
+    chunk = min(rows, 2048)
     chunks = rows // chunk
     plan = Plan(panels, tiles, blocks)
     width = min(slice_width, BLK)
     params = pltpu.CompilerParams(vmem_limit_bytes=VMEM_BYTES)
 
-    table, sent, spread = pl.pallas_call(
-        functools.partial(prep_kernel, plan, group),
-        in_specs=[SMEM, VMEM, ANY, ANY],
-        out_specs=(SMEM, ANY, VMEM),
+    sent = pl.pallas_call(
+        functools.partial(pack_kernel, group),
+        in_specs=[ANY, ANY],
+        out_specs=ANY,
+        out_shape=jax.ShapeDtypeStruct((BLK, virt_count + occ_count), jnp.bfloat16),
+        scratch_shapes=[pltpu.SemaphoreType.DMA((2,))],
+        compiler_params=params,
+        name="pack",
+    )(occupied_orbitals, virtual_orbitals)
+    table, spread = pl.pallas_call(
+        functools.partial(plan_kernel, plan, group),
+        in_specs=[ANY, ANY, ANY],
+        out_specs=(SMEM, VMEM),
         out_shape=(
             jax.ShapeDtypeStruct((plan.size,), jnp.int32),
-            jax.ShapeDtypeStruct((BLK, virt_count + occ_count), jnp.bfloat16),
             jax.ShapeDtypeStruct((count_ta, slice_width // width, NVEC, width), jnp.bfloat16),
         ),
         scratch_shapes=[
-            pltpu.SMEM((2 * blocks,), jnp.int32),
-            pltpu.SMEM((blocks,), jnp.int32),
+            pltpu.SMEM(tile_columns.shape, jnp.int32),
+            pltpu.VMEM(probe_vectors.shape, jnp.bfloat16),
+            pltpu.SMEM((2, blocks), jnp.int32),
+            pltpu.SMEM((2, blocks), jnp.int32),
             pltpu.SemaphoreType.DMA((2,)),
         ],
         compiler_params=params,
-        name="prep",
-    )(tile_columns, probe_vectors, occupied_orbitals, virtual_orbitals)
+        name="plan",
+    )(tile_columns, probe_vectors, sent)
 
     others = [
         lax.ppermute(sent, "pa", [(q, (q - offset) % panels) for q in range(panels)])
@@ -450,7 +466,7 @@
     )(table, times, occupied_gaps, virtual_gaps, occupied_orbitals, virtual_orbitals)
 
     partial_response = pl.pallas_call(
-        functools.partial(rest_kernel, plan, chunk),
+        functools.partial(rest_kernel, plan, rows),
         in_specs=[SMEM, SMEM, SMEM, VMEM, VMEM, ANY, ANY, ANY, ANY, VMEM],
         out_specs=VMEM,
         out_shape=jax.ShapeDtypeStruct((count_ta * panels, NVEC, BLK), jnp.float32),

time: 74 us -> 69.3 us (0.936)
  Pallas kernels: 42.9 us -> 37.2 us
  blocking collectives: 19.9 us -> 22.1 us
  local copies, waits for them, and re-layouts: 1.51 us -> 0.09 us
    pallas_call x1, Pallas kernels: 18.4 us -> 10.7 us  [shards(): pl.pallas_call(functools.partial(own_kernel, plan, chunk), in_specs=[SMEM...]
    all_to_all x1, blocking collectives: 19.9 us -> 22.1 us  [shards(): parts = lax.all_to_all(partial_response, ('ta', 'pa'), 0, 0, tiled=True)]
    pallas_call x2 -> x3, Pallas kernels: 23.1 us -> 25.1 us  [the longest x1 20.8 us: shards(): pl.pallas_call(functools.partial(rest_kernel, plan, rows), in_specs=[SMEM...]
    unnamed x7 -> x9, local copies, waits for them, and re-layouts: 1.51 us -> 0.09 us
    ppermute x1, starting transfers between devices: 1.24 us -> 2.13 us  [shards(): lax.ppermute(sent, 'pa', [(q, (q - offset) % panels) for q in range(panel...]
  transfers between devices with their start and end apart: 2 -> 2, of which waited for: 0 -> 0; matrix products, arithmetic and copies ran while one was open for 0% -> 0% of each run, Pallas kernels for 25% -> 20%
where the time goes in v1:
time: 69.3 us; the launch traced here: 68.5 us
  Pallas kernels  37.2 us (54%)
  blocking collectives  22.1 us (32%)
  starting transfers between devices  8.92 us (13%)
    all_to_all x1, blocking collectives, shards(): parts = lax.all_to_all(partial_response, ('ta', 'pa'), 0, 0, tiled=True)  22.1 us
    pallas_call x1, Pallas kernels, shards(): pl.pallas_call(functools.partial(rest_kernel, plan, rows), in_specs=[SMEM...  20.8 us
    pallas_call x1, Pallas kernels, shards(): pl.pallas_call(functools.partial(own_kernel, plan, chunk), in_specs=[SMEM...  10.7 us
    all_to_all x1, starting transfers between devices, shards(): probes = lax.all_to_all(spread, 'ta', 0, 0, tiled=True)  6.78 us
    pallas_call x1, Pallas kernels, shards(): pl.pallas_call(functools.partial(plan_kernel, plan, group), in_specs=[ANY...  3.23 us
    ppermute x1, starting transfers between devices, shards(): lax.ppermute(sent, 'pa', [(q, (q - offset) % panels) for q in range(panel...  2.13 us
  transfers between devices with their start and end apart: 2, of which 0 were waited for; matrix products, arithmetic and copies ran while one was open for 0% of the time, Pallas kernels for 20%

profile of v1, /device:TPU:1, one launch (start us, length us, event | category | flops | bytes accessed | tf_op | source)
XLA Modules:
  0.0 68.5 jit_solution(5936342367366623305)
XLA Ops:
  0.0 0.0 copy-start.3
  0.0 0.0 copy-start
  0.0 0.0 copy-start.1
  0.0 0.0 copy-start.2
  0.0 1.1 %pack.1.after = bf16[128,2048]{1,0:T(8,128)(2,1)S(1)} custom-call(bf16[2048,512]{1,0:T(8,128)(2,1)} %occ.5, bf16[2048,1536]{1,0:T(8,128)(2,1)} %virt.5), custom_call_target="tpu_custom_call" | custom-call | tf_op jit(solution)/shard_map/pack/pallas_call | solution.py:399
  1.1 2.1 %collective-permute-start = (bf16[128,2048]{1,0:T(8,128)(2,1)S(1)}, bf16[128,2048]{1,0:T(8,128)(2,1)S(1)}, u32[]{:S(2)}, u32[]{:S(2)}) collective-permute-start(bf16[128,2048]{1,0:T(8,128)(2,1)S(1)} %pack.1.after), channel_id=1, source_target_pairs={{0,1},{1,0},{2,3},{3,2},{4,5},{5,4},{6,7},{7,6},{8,9},{9,8},{10,11... | collective-permute-start | bytes 1572872 | tf_op jit(solution)/shard_map/ppermute | solution.py:428
  3.2 0.0 copy-done.3
  3.2 0.1 copy.7.tiles_hbm
  3.3 0.0 copy-done
  3.3 3.2 %plan.1 = (s32[34]{0:T(128)S(1)}, bf16[16,2,32,128]{3,2,1,0:T(8,128)(2,1)}) custom-call(s32[32,8]{1,0:T(8,128)S(1)} %copy.7.tiles_hbm, bf16[32,256]{1,0:T(8,128)(2,1)S(1)} %copy-done, bf16[128,2048]{1,0:T(8,128)(2,1)S(1)} %pack.1.after), custom_call_target="tpu_custom_call" | custom-call | tf_op jit(solution)/shard_map/plan/pallas_call | solution.py:408
  6.6 6.8 %all-to-all-start = ((bf16[16,2,32,128]{3,2,1,0:T(8,128)(2,1)}), bf16[16,2,32,128]{3,2,1,0:T(8,128)(2,1)S(1)}, u32[]{:S(2)}, u32[]{:S(2)}) async-start(bf16[16,2,32,128]{3,2,1,0:T(8,128)(2,1)} %get-tuple-element.8), calls=%async_computation | async-start | bytes 524288 | tf_op jit(solution)/shard_map/all_to_all | solution.py:433
  13.4 0.0 copy-done.1
  13.4 0.0 copy-done.2
  13.4 10.7 %own_tiles.1.polar = bf16[1024,4096]{1,0:T(8,128)(2,1)} custom-call(s32[34]{0:T(128)S(1)} %get-tuple-element.7.table, f32[32]{0:T(128)S(1)} %get-tuple-element.9.times, f32[512]{0:T(512)S(1)} %copy-done.2, f32[1536]{0:T(1024)S(1)} %copy-done.1, bf16[2048,512]{1,0:T(8,128)(2,1)} %occ.5, bf16[2048,1536]{1,0:T(8,128)(2,1)} %virt.5), custom_call_target="tpu_custom_call" | custom-call | flops 8589934592 | bytes 8388608 | tf_op jit(solution)/shard_map/own_tiles/pallas_call | solution.py:457
  24.1 0.1 cosine_multiply_fusion.cosine
  24.2 0.0 all-to-all-done
  24.3 0.0 collective-permute-done.other_rows
  24.3 20.8 %other_tiles.1 = f32[32,32,128]{2,1,0:T(8,128)S(1)} custom-call(s32[34]{0:T(128)S(1)} %get-tuple-element.7.table, f32[32]{0:T(128)S(1)} %get-tuple-element.9.times, f32[16,32]{1,0:T(8,128)S(1)} %cosine_multiply_fusion.cosine, f32[512]{0:T(512)S(1)} %copy-done.2, f32[1536]{0:T(1024)S(1)} %copy-done.1, bf16[128,2048]{1,0:T(8,128)(2,1)S(1)} %collective-permute-done.other_rows, ...), custom_call_target="tpu_custom_call" | custom-call | flops 8589934592 | bytes 8388608 | tf_op jit(solution)/shard_map/other_tiles/pallas_call | solution.py:468
  45.1 22.1 %all_to_all.10.parts = f32[32,32,128]{2,1,0:T(8,128)S(1)} all-to-all(f32[32,32,128]{2,1,0:T(8,128)S(1)} %other_tiles.1), channel_id=1, replica_groups=mesh['ta'=16,'pa'=2] {'ta','pa'}, dimensions={0} | all-to-all | bytes 1048576 | tf_op jit(solution)/shard_map/all_to_all | solution.py:489
  67.2 1.3 %sum_parts.1 = f32[1,32,2048]{2,1,0:T(8,128)} custom-call(s32[34]{0:T(128)S(1)} %get-tuple-element.7.table, f32[32,32,128]{2,1,0:T(8,128)S(1)} %all_to_all.10.parts), custom_call_target="tpu_custom_call" | custom-call | tf_op jit(solution)/shard_map/sum_parts/pallas_call | solution.py:490
  (2 shorter events, 0.0 us)
Async XLA Ops:
  0.0 3.2 %copy-start.3 = (s32[32,8]{0,1:T(8,128)S(1)}, s32[32,8]{0,1:T(8,128)}, u32[]{:S(2)}) copy-start(s32[32,8]{0,1:T(8,128)} %param.10) | copy-start | bytes 3076
  0.0 3.3 %copy-start = (bf16[32,256]{1,0:T(8,128)(2,1)S(1)}, bf16[32,256]{1,0:T(8,128)(2,1)}, u32[]{:S(2)}) copy-start(bf16[32,256]{1,0:T(8,128)(2,1)} %probe_hbm.1) | copy-start | bytes 49156
  0.0 13.4 %copy-start.1 = (f32[1536]{0:T(1024)S(1)}, f32[1536]{0:T(1024)}, u32[]{:S(2)}) copy-start(f32[1536]{0:T(1024)} %gaps_virt.3) | copy-start | bytes 18436
  0.0 13.4 %copy-start.2 = (f32[512]{0:T(512)S(1)}, f32[512]{0:T(512)}, u32[]{:S(2)}) copy-start(f32[512]{0:T(512)} %gaps_occ.3) | copy-start | bytes 6148
  1.1 23.1 %collective-permute-start = (bf16[128,2048]{1,0:T(8,128)(2,1)S(1)}, bf16[128,2048]{1,0:T(8,128)(2,1)S(1)}, u32[]{:S(2)}, u32[]{:S(2)}) collective-permute-start(bf16[128,2048]{1,0:T(8,128)(2,1)S(1)} %pack.1.after), channel_id=1, source_target_pairs={{0,1},{1,0},{2,3},{3,2},{4,5},{5,4},{6,7},{7,6},{8,9},{9,8},{10,11... | collective-permute-start | bytes 1572872 | tf_op jit(solution)/shard_map/ppermute | solution.py:428
  6.6 17.7 %all-to-all-start = ((bf16[16,2,32,128]{3,2,1,0:T(8,128)(2,1)}), bf16[16,2,32,128]{3,2,1,0:T(8,128)(2,1)S(1)}, u32[]{:S(2)}, u32[]{:S(2)}) async-start(bf16[16,2,32,128]{3,2,1,0:T(8,128)(2,1)} %get-tuple-element.8), calls=%async_computation | async-start | bytes 524288 | tf_op jit(solution)/shard_map/all_to_all | solution.py:433
